TPU v7x, 128 devices: a whole 4x4x4 slice. The times are simulated.
128 devices in a mesh: dp: 32 (over z, y, core), mp: 4 (over x).
Axes of the slice: x: 4, y: 4, z: 4, core: 2. Of those that a mesh axis runs over, the one named last changes fastest.
Arguments:
- features: bfloat16 [262144, 512], P('dp', 'mp'), may hold values from -6 to 6
- conv6_weight: bfloat16 [1024, 512], P('dp', 'mp'), may hold values from -0.1875 to 0.1875
- conv7_weight: bfloat16 [1024, 512], P('dp', 'mp'), may hold values from -0.1875 to 0.1875
- frame_grads: bfloat16 [65536, 512], P('dp', 'mp'), may hold values from -0.29882812 to 0.29882812
- frame_dest: int32 [65536], replicated, may hold values from 0 to 65535, as said below
- lengths: int32 [128], P('dp'), may hold values from 41360 to 163920
Outputs:
- grad_features: bfloat16 [262144, 512], P('dp', 'mp')
- grad_conv6: float32 [1024, 512], P('dp', 'mp')
- grad_conv7: float32 [1024, 512], P('dp', 'mp')
Inputs may be any that keep to these rules, and one draw needn't show every extreme that they name: frame_dest maps the packed slots one to one onto all waveform frames; frame f belongs to the waveform owner f // 2048, slot j lies on transformer owner j // 2048. Every transformer owner sends at most 192 frames to one waveform owner and exactly 192 to one of them; every waveform owner receives exactly 192 frames from one transformer owner. `lengths`: entry d * 4 + u belongs to the utterance in output frames (d * 4 + u) * 512 onward.
All inputs are finite; a program needn't handle non-finite values.
Results may differ from a plain program's by a relative error of at most 0.006.
Values may be sent and summed in bfloat16 or wider, within the bound.
A program may use at most 128 MiB of HBM per device.

v0:
```python
import jax
import jax.numpy as jnp
from jax import lax
from jax.sharding import PartitionSpec as P

inv_root_two = 0.7071067811865476
inv_root_tau = 0.3989422804014327


def gelu_exact(values):
    return 0.5 * values * (1.0 + jax.scipy.special.erf(values * inv_root_two))


def gelu_slope(values):
    return (
        0.5 * (1.0 + jax.scipy.special.erf(values * inv_root_two))
        + values * jnp.exp(-0.5 * values * values) * inv_root_tau
    )


def reduce_kernel(left, right):
    return lax.psum_scatter(
        lax.dot_general(left, right, (((0,), (0,)), ((), ())), preferred_element_type=jnp.float32),
        "dp",
        scatter_dimension=0,
        tiled=True,
    )


def times_transpose(left, right):
    return lax.dot_general(
        left, right, (((1,), (1,)), ((), ())), preferred_element_type=jnp.float32
    )


def join_channels(values):
    return lax.all_gather(values, "mp", axis=1, tiled=True)


def spread_channels(values):
    return lax.psum_scatter(values, "mp", scatter_dimension=1, tiled=True)


def route_frames(frame_grads, frame_dest, lengths):
    dp_count = lax.axis_size("dp")
    own_index = lax.axis_index("dp")
    frames = frame_grads.shape[0]
    capacity = 3 * frames // dp_count
    own_slots = lax.dynamic_slice_in_dim(frame_dest, own_index * frames, frames, 0)
    own_dest = own_slots // frames
    own_rows = own_slots % frames
    owner_ids = jnp.arange(dp_count, dtype=jnp.int32)
    counts = jnp.sum((own_dest[:, None] == owner_ids[None, :]).astype(jnp.int32), axis=0)
    starts = jnp.cumsum(counts) - counts
    grouped = jnp.argsort(own_dest, stable=True)
    bucket_pos = jnp.arange(capacity, dtype=jnp.int32)[None, :]
    filled = bucket_pos < counts[:, None]
    pick_index = jnp.minimum(starts[:, None] + bucket_pos, frames - 1)
    source_row = grouped[pick_index]
    outbox = jnp.where(filled[:, :, None], frame_grads[source_row], jnp.zeros((), jnp.bfloat16))
    target_rows = jnp.where(filled, own_rows[source_row], frames)
    arrived, arrived_rows = (
        lax.all_to_all(outbox, "dp", split_axis=0, concat_axis=0, tiled=True),
        lax.all_to_all(target_rows, "dp", split_axis=0, concat_axis=0, tiled=True),
    )
    placing = jnp.argsort(arrived_rows.reshape(-1), stable=True)[:frames]
    routed = arrived.reshape(dp_count * capacity, arrived.shape[2])[placing]
    valid_len = (lengths - 400) // 320 + 1
    utter_len = frames // lengths.shape[0]
    positions = jnp.arange(frames, dtype=jnp.int32)
    limits = jnp.repeat(valid_len, utter_len, total_repeat_length=frames)
    live_mask = positions % utter_len < limits
    return jnp.where(live_mask[:, None], routed, jnp.zeros_like(routed))


def body(features, conv6_weight, conv7_weight, frame_grads, frame_dest, lengths):
    masked = route_frames(frame_grads, frame_dest, lengths)
    weight_six, weight_seven = (
        lax.all_gather(conv6_weight, "dp", axis=0, tiled=True),
        lax.all_gather(conv7_weight, "dp", axis=0, tiled=True),
    )
    frames = frame_grads.shape[0]
    full_width = weight_six.shape[0] // 2
    joined = join_channels(features)
    in_pairs = joined.reshape(joined.shape[0] // 2, 2 * joined.shape[1])
    pre_six = jnp.dot(in_pairs, weight_six, preferred_element_type=jnp.float32)
    act_six = gelu_exact(pre_six).astype(jnp.bfloat16)
    joined_six = join_channels(act_six)
    six_pairs = joined_six.reshape(frames, 2 * joined_six.shape[1])
    pre_seven = jnp.dot(six_pairs, weight_seven, preferred_element_type=jnp.float32)
    delta_seven = (masked.astype(jnp.float32) * gelu_slope(pre_seven)).astype(jnp.bfloat16)
    grad_seven = reduce_kernel(six_pairs, delta_seven)
    back_six = spread_channels(
        times_transpose(delta_seven, weight_seven).reshape(2 * frames, full_width)
    )
    delta_six = (back_six * gelu_slope(pre_six)).astype(jnp.bfloat16)
    grad_six = reduce_kernel(in_pairs, delta_six)
    back_in = spread_channels(
        times_transpose(delta_six, weight_six).reshape(4 * frames, full_width)
    )
    grad_features = back_in.astype(jnp.bfloat16)
    return (grad_features, grad_six, grad_seven)


def solution(mesh):
    placed = (P("dp", "mp"), P("dp", "mp"), P("dp", "mp"), P("dp", "mp"), P(), P("dp"))
    return jax.shard_map(
        body,
        mesh=mesh,
        in_specs=placed,
        out_specs=(P("dp", "mp"), P("dp", "mp"), P("dp", "mp")),
        check_vma=False,
    )
```

profile of v0, /device:TPU:0, one launch (start us, length us, event | category | flops | bytes accessed | tf_op | source)
XLA Modules:
  0.0 735.1 jit_solution(9145920384795812149)
XLA Ops:
  7.2 0.0 copy-start
  7.2 0.0 all-gather.3.cloned.1.call-start
  7.2 0.7 all-gather.3.cloned.1.call-update
  7.9 0.0 all-gather.5.cloned.1.call-start
  8.0 26.4 %all_gather.13 = bf16[1024,128]{1,0:T(8,128)(2,1)S(1)} all-gather(bf16[32,128]{1,0:T(8,128)(2,1)S(1)} %copy-done.4), channel_id=1, replica_groups=mesh['dp'=32,'mp'=4] {'dp'}, dimensions={0}, use_global_device_ids=true | all-gather | bytes 270336 | tf_op jit(solution)/shard_map/all_gather | solution.py:79
  34.4 65.2 %all-gather.3.cloned.1.call-done = bf16[8192,512]{1,0:T(8,128)(2,1)} async-done(((bf16[8192,128]{1,0:T(8,128)(2,1)}), bf16[8192,512]{1,0:T(8,128)(2,1)}) %all-gather.3.cloned.1.call-update) | async-done | bytes 8388624 | tf_op jit(solution)/shard_map/all_gather | solution.py:37
  99.6 12.9 %reshape.258 = bf16[4096,1024]{1,0:T(8,128)(2,1)} reshape(bf16[8192,512]{1,0:T(8,128)(2,1)} %all-gather.3.cloned.1.call-done) | data formatting | bytes 16777216 | tf_op jit(solution)/shard_map/reshape | solution.py:85
  112.5 7.4 %multiply_convert_fusion = (bf16[4096,128]{1,0:T(8,128)(2,1)}, f32[4096,128]{1,0:T(8,128)}) fusion(bf16[4096,1024]{1,0:T(8,128)(2,1)} %reshape.258, bf16[1024,128]{1,0:T(8,128)(2,1)S(1)} %all_gather.13), kind=kOutput, calls=%fused_computation.11 | convolution fusion | flops 1076363264 | bytes 11796480 | tf_op jit(solution)/shard_map/dot_general | solution.py:86
  119.9 0.0 all-gather.5.cloned.1.call-update
  119.9 0.7 add_select_fusion
  120.6 0.7 add_select_fusion.1
  121.3 5.0 sort.34
  126.4 0.1 convert_reduce_fusion
  126.5 0.1 copy.15
  126.6 0.1 reduce-window.12
  126.7 0.1 reduce.2
  126.8 0.1 compare_select_fusion.2
  126.9 0.1 reshape.275
  127.0 34.3 %gather_fusion = s32[6144]{0:T(1024)S(1)} fusion(s32[2048]{0:T(1024)S(1)} %get-tuple-element.17, s32[6144]{0:T(1024)S(1)} %broadcast_clamp_fusion), kind=kCustom, calls=%fused_computation | custom fusion | bytes 73728 | tf_op jit(solution)/shard_map/gather | solution.py:59
  161.3 0.1 gather.22
  161.3 0.1 reshape.283
  161.4 34.3 %gather_fusion.2 = s32[6144]{0:T(1024)S(1)} fusion(s32[2048]{0:T(1024)S(1)} %get-tuple-element.31, s32[6144]{0:T(1024)S(1)} %broadcast_clamp_fusion.1), kind=kCustom, calls=%fused_computation.2 | custom fusion | bytes 73728 | tf_op jit(solution)/shard_map/gather | solution.py:61
  195.7 0.1 gather.25
  195.8 0.7 compare_select_fusion
  196.5 7.3 all-to-all-start.1
  203.8 18.1 %gather_fusion.1 = bf16[6144,128]{1,0:T(8,128)(2,1)S(1)} fusion(bf16[2048,128]{1,0:T(8,128)(2,1)S(1)} %copy-done, s32[6144]{0:T(1024)S(1)} %broadcast_clamp_fusion.1), kind=kCustom, calls=%fused_computation.1 | custom fusion | bytes 3170304 | tf_op jit(solution)/shard_map/gather | solution.py:60
  221.9 0.1 iota_compare_fusion.1
  222.0 2.3 broadcast_select_fusion
  224.3 0.0 copy-start.8
  224.4 0.0 all-to-all-done.1
  224.4 7.5 %all-to-all-start = ((bf16[32,192,128]{2,1,0:T(8,128)(2,1)}), bf16[32,192,128]{2,1,0:T(8,128)(2,1)S(1)}, u32[]{:S(2)}, u32[]{:S(2)}) async-start(bf16[32,192,128]{2,1,0:T(8,128)(2,1)} %broadcast_select_fusion), calls=%async_computation | async-start | bytes 3145728 | tf_op jit(solution)/shard_map/all_to_all | solution.py:63
  231.9 0.0 reduce-scatter.7.cloned.1.call-start
  232.0 38.6 %all_gather.15 = bf16[1024,128]{1,0:T(8,128)(2,1)S(1)} all-gather(bf16[32,128]{1,0:T(8,128)(2,1)S(1)} %copy-done.5), channel_id=1, replica_groups=mesh['dp'=32,'mp'=4] {'dp'}, dimensions={0}, use_global_device_ids=true | all-gather | bytes 270336 | tf_op jit(solution)/shard_map/all_gather | solution.py:80
  270.6 0.7 fusion.26
  271.3 2.5 fusion.12
  273.8 0.1 reduce.3
  273.9 0.1 reshape.257
  274.0 6.7 sort.35
  280.7 0.0 all-to-all-done
  280.7 6.2 gather_fusion.3
  286.9 0.0 all-gather.5.cloned.1.call-done
  287.0 7.1 reshape.259
  294.0 3.5 fusion.27
  297.5 1.0 copy-done.3
  298.5 4.0 fusion.21
  302.5 9.3 %reshape.260 = f32[4096,512]{1,0:T(8,128)} reshape(f32[2048,1024]{1,0:T(8,128)} %fusion.21) | data formatting | bytes 16777216 | tf_op jit(solution)/shard_map/reshape | solution.py:94
  311.9 0.0 reduce-scatter.7.cloned.1.call-update
  311.9 0.0 reduce-scatter.9.cloned.1.call-start
  311.9 78.9 %reduce-scatter.7.cloned.1.call-done = f32[4096,128]{1,0:T(8,128)} async-done(((f32[4096,512]{1,0:T(8,128)}), f32[4096,128]{1,0:T(8,128)}) %reduce-scatter.7.cloned.1.call-update) | async-done | bytes 2097168 | tf_op jit(solution)/shard_map/reduce_scatter | solution.py:41
  390.8 9.7 %fusion.24 = f32[4096,1024]{1,0:T(8,128)} fusion(bf16[1024,128]{1,0:T(8,128)(2,1)S(1)} %all_gather.13, f32[4096,128]{1,0:T(8,128)} %reduce-scatter.7.cloned.1.call-done, f32[4096,128]{1,0:T(8,128)S(1)} %copy-done.2), kind=kOutput, calls=%fused_computation.51 | convolution fusion | flops 1078984704 | bytes 21233664 | tf_op jit(solution)/shard_map/dot_general | solution.py:31
  400.5 18.2 %reshape.261 = f32[8192,512]{1,0:T(8,128)} reshape(f32[4096,1024]{1,0:T(8,128)} %fusion.24) | data formatting | bytes 33554432 | tf_op jit(solution)/shard_map/reshape | solution.py:99
  418.6 0.0 reduce-scatter.9.cloned.1.call-update
  418.7 0.0 reduce-scatter.11.cloned.1.call-start
  418.7 4.9 fusion.19
  423.7 0.0 reduce-scatter.11.cloned.1.call-update
  423.7 0.0 reduce-scatter.13.cloned.1.call-start
  423.7 6.6 convolution_bitcast_fusion
  430.3 1.0 copy.17
  431.4 0.0 reduce-scatter.13.cloned.1.call-update
  431.4 0.0 copy-start.1
  431.4 135.1 %reduce-scatter.9.cloned.1.call-done = f32[8192,128]{1,0:T(8,128)} async-done(((f32[8192,512]{1,0:T(8,128)}), f32[8192,128]{1,0:T(8,128)}) %reduce-scatter.9.cloned.1.call-update) | async-done | bytes 4194320 | tf_op jit(solution)/shard_map/reduce_scatter | solution.py:41
  566.5 3.7 convert_element_type.23
  570.2 77.5 %reduce-scatter.11.cloned.1.call-done = f32[32,128]{1,0:T(8,128)} async-done(((f32[1024,128]{1,0:T(8,128)}), f32[32,128]{1,0:T(8,128)}) %reduce-scatter.11.cloned.1.call-update) | async-done | bytes 16400 | tf_op jit(solution)/shard_map/reduce_scatter | solution.py:22
  647.6 80.6 %reduce-scatter.13.cloned.1.call-done = f32[32,128]{1,0:T(8,128)} async-done(((f32[1024,128]{1,0:T(8,128)}), f32[32,128]{1,0:T(8,128)}) %reduce-scatter.13.cloned.1.call-update) | async-done | bytes 16400
  (24 shorter events, 0.1 us)
Async XLA Ops:
  7.2 196.6 %copy-start = (bf16[2048,128]{1,0:T(8,128)(2,1)S(1)}, bf16[2048,128]{1,0:T(8,128)(2,1)}, u32[]{:S(2)}) copy-start(bf16[2048,128]{1,0:T(8,128)(2,1)} %param.11) | copy-start | bytes 1572868
  7.2 0.8 copy-start.4
  7.2 92.4 %all-gather.3.cloned.1.call-start = ((), (), s32[]{:S(2)}) async-start(), calls=%async_computation.6 | async-start | bytes 10485760 | tf_op jit(solution)/shard_map/all_gather | solution.py:37
  7.9 279.0 %all-gather.5.cloned.1.call-start = ((), (), s32[]{:S(2)}) async-start(), calls=%async_computation.7 | async-start | bytes 5242880 | tf_op jit(solution)/shard_map/all_gather | solution.py:37
  196.5 27.8 %all-to-all-start.1 = ((s32[32,1,192]{2,1,0:T(1,128)}), s32[32,1,192]{2,1,0:T(1,128)S(1)}, u32[]{:S(2)}, u32[]{:S(2)}) async-start(s32[32,1,192]{2,1,0:T(1,128)} %compare_select_fusion), calls=%async_computation.1 | async-start | bytes 65536 | tf_op jit(solution)/shard_map/all_to_all | solution.py:64
  224.3 7.6 %copy-start.5 = (bf16[32,128]{1,0:T(8,128)(2,1)S(1)}, bf16[32,128]{1,0:T(8,128)(2,1)}, u32[]{:S(2)}) copy-start(bf16[32,128]{1,0:T(8,128)(2,1)} %param.10) | copy-start | bytes 24580
  224.3 46.2 %copy-start.9 = (s32[4]{0:T(128)S(1)}, s32[4]{0:T(128)}, u32[]{:S(2)}) copy-start(s32[4]{0:T(128)} %param.13) | copy-start | bytes 52
  224.3 46.9 %copy-start.6 = (pred[2048]{0:T(1024)(128)(4,1)S(1)}, pred[2048]{0:T(1024)(128)(4,1)}, u32[]{:S(2)}) copy-start(pred[2048]{0:T(1024)(128)(4,1)} %constant.191) | copy-start | bytes 6148
  224.3 46.9 %copy-start.7 = (pred[2048]{0:T(1024)(128)(4,1)S(1)}, pred[2048]{0:T(1024)(128)(4,1)}, u32[]{:S(2)}) copy-start(pred[2048]{0:T(1024)(128)(4,1)} %constant.190) | copy-start | bytes 6148
  224.3 46.9 %copy-start.8 = (pred[2048]{0:T(1024)(128)(4,1)S(1)}, pred[2048]{0:T(1024)(128)(4,1)}, u32[]{:S(2)}) copy-start(pred[2048]{0:T(1024)(128)(4,1)} %constant.189) | copy-start | bytes 6148
  224.4 56.4 %all-to-all-start = ((bf16[32,192,128]{2,1,0:T(8,128)(2,1)}), bf16[32,192,128]{2,1,0:T(8,128)(2,1)S(1)}, u32[]{:S(2)}, u32[]{:S(2)}) async-start(bf16[32,192,128]{2,1,0:T(8,128)(2,1)} %broadcast_select_fusion), calls=%async_computation | async-start | bytes 3145728 | tf_op jit(solution)/shard_map/all_to_all | solution.py:63
  231.9 158.9 %reduce-scatter.7.cloned.1.call-start = ((), (), s32[]{:S(2)}) async-start(), calls=%async_computation.8 | async-start | bytes 10485760 | tf_op jit(solution)/shard_map/reduce_scatter | solution.py:41
  297.5 1.0 copy-start.3
  311.8 79.0 %copy-start.2 = (f32[4096,128]{1,0:T(8,128)S(1)}, f32[4096,128]{1,0:T(8,128)}, u32[]{:S(2)}) copy-start(f32[4096,128]{1,0:T(8,128)} %get-tuple-element.38) | copy-start | bytes 6291460
  311.9 254.6 %reduce-scatter.9.cloned.1.call-start = ((), (), s32[]{:S(2)}) async-start(), calls=%async_computation.9 | async-start | bytes 20971520 | tf_op jit(solution)/shard_map/reduce_scatter | solution.py:41
  418.7 229.0 %reduce-scatter.11.cloned.1.call-start = ((), (), s32[]{:S(2)}) async-start(), calls=%async_computation.10 | async-start | bytes 540672 | tf_op jit(solution)/shard_map/reduce_scatter | solution.py:22
  423.7 304.5 %reduce-scatter.13.cloned.1.call-start = ((), (), s32[]{:S(2)}) async-start(), calls=%async_computation.11 | async-start | bytes 540672
  431.4 296.8 %copy-start.1 = (bf16[2048,128]{1,0:T(8,128)(2,1)S(1)}, bf16[2048,128]{1,0:T(8,128)(2,1)}, u32[]{:S(2)}) copy-start(bf16[2048,128]{1,0:T(8,128)(2,1)} %param.11) | copy-start | bytes 1572868
Sparse Core Ops, SparseCore 0:
  9.7 89.8 all-gather.2
  120.0 52.3 all-gather.4
  312.0 78.7 reduce-scatter.6
  418.8 147.6 reduce-scatter.8
  570.7 76.8 reduce-scatter.10
  651.9 76.2 reduce-scatter.12
where the time goes:
time: 737 us; the launch traced here: 735 us
  waiting for transfers between devices  438 us (59%)
  local copies, waits for them, and re-layouts  144 us (20%)
  blocking collectives  65 us (9%)
  matrix products  36.1 us (5%)
  other arithmetic  23.1 us (3%)
  starting transfers between devices  15 us (2%)
  between operations  14.3 us (2%)
    reduce_scatter x2, waiting for transfers between devices, spread_channels(): return lax.psum_scatter(values, 'mp', scatter_dimension=1, tiled=True)  214 us
    unnamed x7, waiting for transfers between devices  81.4 us
    reduce_scatter x1, waiting for transfers between devices, reduce_kernel(): lax.psum_scatter(lax.dot_general(left, right, (((0,), (0,)), ((), ())), p...  77.5 us
    all_gather x2, waiting for transfers between devices, join_channels(): return lax.all_gather(values, 'mp', axis=1, tiled=True)  65.2 us
    all_gather x1, blocking collectives, body(): lax.all_gather(conv7_weight, 'dp', axis=0, tiled=True)  38.6 us
    gather x2, local copies, waits for them, and re-layouts, route_frames(): target_rows = jnp.where(filled, own_rows[source_row], frames)  34.4 us
    gather x2, local copies, waits for them, and re-layouts, route_frames(): source_row = grouped[pick_index]  34.4 us
    all_gather x1, blocking collectives, body(): lax.all_gather(conv6_weight, 'dp', axis=0, tiled=True)  26.4 us
  transfers between devices with their start and end apart: 8, of which 5 were waited for; matrix products, arithmetic and copies ran while one was open for 18% of the time, Pallas kernels for 0%

commit v1 on v0

--- a/solution.py
+++ b/solution.py
@@ -34,7 +34,9 @@
 
 
 def join_channels(values):
-    return lax.all_gather(values, "mp", axis=1, tiled=True)
+    return jnp.concatenate(
+        lax.all_to_all(jnp.stack([values] * lax.axis_size("mp")), "mp", 0, 0), axis=1
+    )
 
 
 def spread_channels(values):

time: 737 us -> 795 us (1.079)
  local copies, waits for them, and re-layouts: 144 us -> 173 us
  waiting for transfers between devices: 438 us -> 454 us
  blocking collectives: 65 us -> 78.7 us
    all_to_all x1 -> x2, waiting for transfers between devices: 0.01 us -> 82.8 us  [join_channels(): lax.all_to_all(jnp.stack([values] * lax.axis_size('mp')), 'mp', 0, 0)]
    all_gather x2 -> x0, waiting for transfers between devices: 65.2 us -> none  [join_channels(): return lax.all_gather(values, 'mp', axis=1, tiled=True)]
    another operation x1 -> x5, local copies, waits for them, and re-layouts: 0.09 us -> 30.1 us  [the longest x1 14.3 us: body(): in_pairs = joined.reshape(joined.shape[0] // 2, 2 * joined.shape[1])]
    all_to_all x0 -> x1, blocking collectives: none -> 15.6 us  [route_frames(): lax.all_to_all(target_rows, 'dp', split_axis=0, concat_axis=0, tiled=True)]
    all_gather x1, blocking collectives: 38.6 us -> 24.4 us  [body(): lax.all_gather(conv7_weight, 'dp', axis=0, tiled=True)]
    all_gather x1, blocking collectives: 26.4 us -> 38.7 us  [body(): lax.all_gather(conv6_weight, 'dp', axis=0, tiled=True)]
    unnamed x7 -> x5, waiting for transfers between devices: 81.4 us -> 80.7 us
  transfers between devices with their start and end apart: 8 -> 7, of which waited for: 5 -> 6; matrix products, arithmetic and copies ran while one was open for 18% -> 11% of each run, Pallas kernels for 0% -> 0%
where the time goes in v1:
time: 795 us; the launch traced here: 793 us
  waiting for transfers between devices  454 us (57%)
  local copies, waits for them, and re-layouts  173 us (22%)
  blocking collectives  78.7 us (10%)
  matrix products  36.3 us (5%)
  other arithmetic  22.5 us (3%)
  starting transfers between devices  15 us (2%)
  between operations  14 us (2%)
    reduce_scatter x2, waiting for transfers between devices, spread_channels(): return lax.psum_scatter(values, 'mp', scatter_dimension=1, tiled=True)  213 us
    all_to_all x2, waiting for transfers between devices, join_channels(): lax.all_to_all(jnp.stack([values] * lax.axis_size('mp')), 'mp', 0, 0)  82.8 us
    unnamed x5, waiting for transfers between devices  80.7 us
    reduce_scatter x1, waiting for transfers between devices, reduce_kernel(): lax.psum_scatter(lax.dot_general(left, right, (((0,), (0,)), ((), ())), p...  77.6 us
    all_gather x1, blocking collectives, body(): lax.all_gather(conv6_weight, 'dp', axis=0, tiled=True)  38.7 us
    gather x2, local copies, waits for them, and re-layouts, route_frames(): target_rows = jnp.where(filled, own_rows[source_row], frames)  34.4 us
    gather x2, local copies, waits for them, and re-layouts, route_frames(): source_row = grouped[pick_index]  34.4 us
    all_gather x1, blocking collectives, body(): lax.all_gather(conv7_weight, 'dp', axis=0, tiled=True)  24.4 us
  transfers between devices with their start and end apart: 7, of which 6 were waited for; matrix products, arithmetic and copies ran while one was open for 11% of the time, Pallas kernels for 0%

profile of v1, /device:TPU:0, one launch (start us, length us, event | category | flops | bytes accessed | tf_op | source)
XLA Modules:
  0.0 793.4 jit_solution(15845729415340580482)
XLA Ops:
  7.2 0.0 copy-start
  7.2 0.8 add_select_fusion
  8.0 0.7 add_select_fusion.1
  8.7 0.1 convert_reduce_fusion
  8.8 5.0 sort.34
  13.8 0.1 copy.17
  13.9 0.1 reduce-window.12
  14.0 0.1 reduce.2
  14.1 0.1 compare_select_fusion.2
  14.2 0.1 reshape.279
  14.3 34.3 %gather_fusion = s32[6144]{0:T(1024)S(1)} fusion(s32[2048]{0:T(1024)S(1)} %get-tuple-element.17, s32[6144]{0:T(1024)S(1)} %broadcast_clamp_fusion), kind=kCustom, calls=%fused_computation | custom fusion | bytes 73728 | tf_op jit(solution)/shard_map/gather | solution.py:61
  48.6 0.1 gather.22
  48.7 0.1 reshape.287
  48.8 0.0 copy-start.4
  48.8 34.3 %gather_fusion.2 = s32[6144]{0:T(1024)S(1)} fusion(s32[2048]{0:T(1024)S(1)} %get-tuple-element.31, s32[6144]{0:T(1024)S(1)} %broadcast_clamp_fusion.1), kind=kCustom, calls=%fused_computation.2 | custom fusion | bytes 73728 | tf_op jit(solution)/shard_map/gather | solution.py:63
  83.1 0.1 gather.25
  83.2 0.1 compare_select_fusion
  83.3 15.6 %all_to_all.21 = s32[32,1,192]{2,1,0:T(1,128)S(1)} all-to-all(s32[32,1,192]{2,1,0:T(1,128)S(1)} %compare_select_fusion), channel_id=1, replica_groups=mesh['dp'=32,'mp'=4] {'dp'}, dimensions={0} | all-to-all | bytes 49152 | tf_op jit(solution)/shard_map/all_to_all | solution.py:66
  98.9 4.3 stack.4
  103.2 5.7 all-to-all-start.2
  108.9 18.1 %gather_fusion.1 = bf16[6144,128]{1,0:T(8,128)(2,1)S(1)} fusion(bf16[2048,128]{1,0:T(8,128)(2,1)S(1)} %copy-done, s32[6144]{0:T(1024)S(1)} %broadcast_clamp_fusion.1), kind=kCustom, calls=%fused_computation.1 | custom fusion | bytes 3170304 | tf_op jit(solution)/shard_map/gather | solution.py:62
  127.0 0.1 iota_compare_fusion.1
  127.0 2.3 broadcast_select_fusion
  129.4 73.8 %all-to-all-done.2 = bf16[4,8192,128]{2,1,0:T(8,128)(2,1)} async-done(((bf16[4,8192,128]{2,1,0:T(8,128)(2,1)}), bf16[4,8192,128]{2,1,0:T(8,128)(2,1)}, u32[]{:S(2)}, u32[]{:S(2)}) %all-to-all-start.2) | async-done | bytes 8388640 | tf_op jit(solution)/shard_map/all_to_all | solution.py:38
  203.2 4.0 all-to-all-start
  207.2 38.7 %all_gather.6 = bf16[1024,128]{1,0:T(8,128)(2,1)S(1)} all-gather(bf16[32,128]{1,0:T(8,128)(2,1)S(1)} %copy-done.5), channel_id=1, replica_groups=mesh['dp'=32,'mp'=4] {'dp'}, dimensions={0}, use_global_device_ids=true | all-gather | bytes 270336 | tf_op jit(solution)/shard_map/all_gather | solution.py:81
  245.9 12.2 %copy.18 = bf16[8192,4,128]{2,1,0:T(4,128)(2,1)} copy(bf16[8192,4,128]{2,0,1:T(8,128)(2,1)} %bitcast.7) | data formatting | bytes 16777216 | tf_op jit(solution)/shard_map/reshape | solution.py:37
  258.0 14.3 %reshape_reshape.6 = bf16[4096,1024]{1,0:T(8,128)(2,1)} reshape(bf16[8192,4,128]{2,1,0:T(4,128)(2,1)} %copy.18) | data formatting | bytes 16777216 | tf_op jit(solution)/shard_map/reshape;reshape | solution.py:87
  272.3 7.4 multiply_convert_fusion
  279.7 3.7 stack.5
  283.5 0.0 copy-start.9
  283.5 5.0 all-to-all-start.3
  288.5 0.0 reduce-scatter.7.cloned.1.call-start
  288.5 24.4 %all_gather.7 = bf16[1024,128]{1,0:T(8,128)(2,1)S(1)} all-gather(bf16[32,128]{1,0:T(8,128)(2,1)S(1)} %copy-done.6), channel_id=1, replica_groups=mesh['dp'=32,'mp'=4] {'dp'}, dimensions={0}, use_global_device_ids=true | all-gather | bytes 270336 | tf_op jit(solution)/shard_map/all_gather | solution.py:82
  313.0 0.6 fusion.26
  313.6 2.5 fusion.12
  316.1 0.1 reduce.3
  316.2 0.1 reshape.261
  316.3 6.7 sort.35
  323.0 6.2 gather_fusion.3
  329.2 8.9 %all-to-all-done.3 = bf16[4,4096,128]{2,1,0:T(8,128)(2,1)} async-done(((bf16[4,4096,128]{2,1,0:T(8,128)(2,1)}), bf16[4,4096,128]{2,1,0:T(8,128)(2,1)}, u32[]{:S(2)}, u32[]{:S(2)}) %all-to-all-start.3) | async-done | bytes 4194336 | tf_op jit(solution)/shard_map/all_to_all | solution.py:38
  338.1 7.6 copy.19
  345.7 7.7 reshape_reshape.7
  353.4 3.5 fusion.27
  356.9 1.0 copy-done.3
  357.9 4.0 fusion.21
  361.9 9.3 %reshape.264 = f32[4096,512]{1,0:T(8,128)} reshape(f32[2048,1024]{1,0:T(8,128)} %fusion.21) | data formatting | bytes 16777216 | tf_op jit(solution)/shard_map/reshape | solution.py:96
  371.2 0.0 reduce-scatter.7.cloned.1.call-update
  371.2 0.0 reduce-scatter.9.cloned.1.call-start
  371.3 78.0 %reduce-scatter.7.cloned.1.call-done = f32[4096,128]{1,0:T(8,128)} async-done(((f32[4096,512]{1,0:T(8,128)}), f32[4096,128]{1,0:T(8,128)}) %reduce-scatter.7.cloned.1.call-update) | async-done | bytes 2097168 | tf_op jit(solution)/shard_map/reduce_scatter | solution.py:43
  449.3 9.7 %fusion.24 = f32[4096,1024]{1,0:T(8,128)} fusion(bf16[1024,128]{1,0:T(8,128)(2,1)S(1)} %all_gather.6, f32[4096,128]{1,0:T(8,128)} %reduce-scatter.7.cloned.1.call-done, f32[4096,128]{1,0:T(8,128)S(1)} %copy-done.2), kind=kOutput, calls=%fused_computation.51 | convolution fusion | flops 1078984704 | bytes 21233664 | tf_op jit(solution)/shard_map/dot_general | solution.py:31
  458.9 18.2 %reshape.265 = f32[8192,512]{1,0:T(8,128)} reshape(f32[4096,1024]{1,0:T(8,128)} %fusion.24) | data formatting | bytes 33554432 | tf_op jit(solution)/shard_map/reshape | solution.py:101
  477.1 0.0 reduce-scatter.9.cloned.1.call-update
  477.1 0.3 reduce-scatter.11.cloned.1.call-start
  477.4 4.9 fusion.19
  482.3 0.0 reduce-scatter.11.cloned.1.call-update
  482.3 0.0 reduce-scatter.13.cloned.1.call-start
  482.4 6.8 convolution_bitcast_fusion
  489.2 1.0 copy.21
  490.2 0.0 reduce-scatter.13.cloned.1.call-update
  490.3 134.6 %reduce-scatter.9.cloned.1.call-done = f32[8192,128]{1,0:T(8,128)} async-done(((f32[8192,512]{1,0:T(8,128)}), f32[8192,128]{1,0:T(8,128)}) %reduce-scatter.9.cloned.1.call-update) | async-done | bytes 4194320 | tf_op jit(solution)/shard_map/reduce_scatter | solution.py:43
  624.9 3.7 convert_element_type.23
  628.6 77.6 %reduce-scatter.11.cloned.1.call-done = f32[32,128]{1,0:T(8,128)} async-done(((f32[1024,128]{1,0:T(8,128)}), f32[32,128]{1,0:T(8,128)}) %reduce-scatter.11.cloned.1.call-update) | async-done | bytes 16400 | tf_op jit(solution)/shard_map/reduce_scatter | solution.py:22
  706.2 80.6 %reduce-scatter.13.cloned.1.call-done = f32[32,128]{1,0:T(8,128)} async-done(((f32[1024,128]{1,0:T(8,128)}), f32[32,128]{1,0:T(8,128)}) %reduce-scatter.13.cloned.1.call-update) | async-done | bytes 16400
  (27 shorter events, 0.1 us)
Async XLA Ops:
  7.2 101.7 %copy-start = (bf16[2048,128]{1,0:T(8,128)(2,1)S(1)}, bf16[2048,128]{1,0:T(8,128)(2,1)}, u32[]{:S(2)}) copy-start(bf16[2048,128]{1,0:T(8,128)(2,1)} %param.11) | copy-start | bytes 1572868
  48.8 50.2 %copy-start.4 = (bf16[8192,128]{1,0:T(8,128)(2,1)S(1)}, bf16[8192,128]{1,0:T(8,128)(2,1)}, u32[]{:S(2)}) copy-start(bf16[8192,128]{1,0:T(8,128)(2,1)} %param.8) | copy-start | bytes 6291460
  103.2 100.0 %all-to-all-start.2 = ((bf16[4,8192,128]{2,1,0:T(8,128)(2,1)}), bf16[4,8192,128]{2,1,0:T(8,128)(2,1)}, u32[]{:S(2)}, u32[]{:S(2)}) async-start(bf16[4,8192,128]{2,1,0:T(8,128)(2,1)} %stack.4), calls=%async_computation.2 | async-start | bytes 16777216 | tf_op jit(solution)/shard_map/all_to_all | solution.py:38
  129.4 77.8 %copy-start.5 = (bf16[32,128]{1,0:T(8,128)(2,1)S(1)}, bf16[32,128]{1,0:T(8,128)(2,1)}, u32[]{:S(2)}) copy-start(bf16[32,128]{1,0:T(8,128)(2,1)} %param.9) | copy-start | bytes 24580
  203.2 76.5 %all-to-all-start = ((bf16[32,192,128]{2,1,0:T(8,128)(2,1)}), bf16[32,192,128]{2,1,0:T(8,128)(2,1)S(1)}, u32[]{:S(2)}, u32[]{:S(2)}) async-start(bf16[32,192,128]{2,1,0:T(8,128)(2,1)} %broadcast_select_fusion), calls=%async_computation | async-start | bytes 3145728 | tf_op jit(solution)/shard_map/all_to_all | solution.py:65
  283.4 5.1 copy-start.6
  283.4 29.5 %copy-start.10 = (s32[4]{0:T(128)S(1)}, s32[4]{0:T(128)}, u32[]{:S(2)}) copy-start(s32[4]{0:T(128)} %param.13) | copy-start | bytes 52
  283.4 30.2 %copy-start.7 = (pred[2048]{0:T(1024)(128)(4,1)S(1)}, pred[2048]{0:T(1024)(128)(4,1)}, u32[]{:S(2)}) copy-start(pred[2048]{0:T(1024)(128)(4,1)} %constant.191) | copy-start | bytes 6148
  283.5 30.2 %copy-start.8 = (pred[2048]{0:T(1024)(128)(4,1)S(1)}, pred[2048]{0:T(1024)(128)(4,1)}, u32[]{:S(2)}) copy-start(pred[2048]{0:T(1024)(128)(4,1)} %constant.190) | copy-start | bytes 6148
  283.5 30.1 %copy-start.9 = (pred[2048]{0:T(1024)(128)(4,1)S(1)}, pred[2048]{0:T(1024)(128)(4,1)}, u32[]{:S(2)}) copy-start(pred[2048]{0:T(1024)(128)(4,1)} %constant.189) | copy-start | bytes 6148
  283.5 54.7 %all-to-all-start.3 = ((bf16[4,4096,128]{2,1,0:T(8,128)(2,1)}), bf16[4,4096,128]{2,1,0:T(8,128)(2,1)}, u32[]{:S(2)}, u32[]{:S(2)}) async-start(bf16[4,4096,128]{2,1,0:T(8,128)(2,1)} %stack.5), calls=%async_computation.3 | async-start | bytes 8388608 | tf_op jit(solution)/shard_map/all_to_all | solution.py:38
  288.5 160.8 %reduce-scatter.7.cloned.1.call-start = ((), (), s32[]{:S(2)}) async-start(), calls=%async_computation.8 | async-start | bytes 10485760 | tf_op jit(solution)/shard_map/reduce_scatter | solution.py:43
  356.9 1.0 copy-start.3
  371.2 78.0 %copy-start.2 = (f32[4096,128]{1,0:T(8,128)S(1)}, f32[4096,128]{1,0:T(8,128)}, u32[]{:S(2)}) copy-start(f32[4096,128]{1,0:T(8,128)} %get-tuple-element.38) | copy-start | bytes 6291460
  371.2 253.6 %reduce-scatter.9.cloned.1.call-start = ((), (), s32[]{:S(2)}) async-start(), calls=%async_computation.9 | async-start | bytes 20971520 | tf_op jit(solution)/shard_map/reduce_scatter | solution.py:43
  477.1 229.1 %reduce-scatter.11.cloned.1.call-start = ((), (), s32[]{:S(2)}) async-start(), calls=%async_computation.10 | async-start | bytes 540672 | tf_op jit(solution)/shard_map/reduce_scatter | solution.py:22
  482.3 304.5 %reduce-scatter.13.cloned.1.call-start = ((), (), s32[]{:S(2)}) async-start(), calls=%async_computation.11 | async-start | bytes 540672
  490.3 296.6 %copy-start.1 = (bf16[2048,128]{1,0:T(8,128)(2,1)S(1)}, bf16[2048,128]{1,0:T(8,128)(2,1)}, u32[]{:S(2)}) copy-start(bf16[2048,128]{1,0:T(8,128)(2,1)} %param.11) | copy-start | bytes 1572868
Sparse Core Ops, SparseCore 0:
  371.4 77.8 reduce-scatter.6
  477.2 147.5 reduce-scatter.8
  629.3 76.8 reduce-scatter.10
  710.4 76.3 reduce-scatter.12
